TPU v7x, 32 devices: a whole 2x2x4 slice. The times are simulated.
32 devices in a mesh: outer: 4 (over x, core), inner: 8 (over z, y).
Axes of the slice: x: 2, y: 2, z: 4, core: 2. Of those that a mesh axis runs over, the one named last changes fastest.
Arguments:
- leaf_q: float32 [8192, 128], P(('outer', 'inner')), may hold values from -0.375 to 0.375
- q_cot: float32 [8192, 128], P(('outer', 'inner')), may hold values from -6 to 6
- leaf_tri: float32 [4096, 128], P(('outer', 'inner')), as said below
- node_blocks: bfloat16 [3, 4096, 128], P(None, ('outer', 'inner')), as said below
- node_tri: bfloat16 [3, 4096, 128], P(None, ('outer', 'inner')), as said below
- root_cot: float32 [128, 128], replicated, may hold values from -6 to 6
Outputs:
- mat_grad: float32 [8192, 128], P(('outer', 'inner'))
Inputs may be any that keep to these rules, and one draw needn't show every extreme that they name: `leaf_tri`: upper triangular; diagonal between 1 and 3. `node_blocks`: at each level, every leaf holds the block of its own child subtree, and all leaves of one child subtree hold equal blocks. `node_tri`: upper triangular with diagonal between 1 and 3; at each level all leaves of one node hold equal triangles.
All inputs are finite; a program needn't handle non-finite values.
Results may differ from a plain program's by a relative error of at most 0.0003.
Values sent between devices are 32-bit elements; how exact they have to be, the bound alone decides.
A program may use at most 64 MiB of HBM per device.

v0:
```python
import jax
import jax.numpy as jnp
from jax import lax
from jax.sharding import PartitionSpec as P

BLOCK = 32


def partner(value, axis, stride):
    mask = 2**stride
    pairs = [(source, source ^ mask) for source in range(lax.axis_size(axis))]
    return lax.ppermute(value, axis, pairs)


def matmul(left_side, right_side):
    return jnp.dot(
        left_side, right_side, precision=lax.Precision.HIGHEST, preferred_element_type=jnp.float32
    )


def inner_product(left_side, right_side):
    return lax.dot_general(
        left_side,
        right_side,
        (((0,), (0,)), ((), ())),
        precision=lax.Precision.HIGHEST,
        preferred_element_type=jnp.float32,
    )


def mirror_lower(matrix):
    return jnp.tril(matrix) + jnp.tril(matrix, -1).T


def small_inverse(block):
    order = block.shape[-1]
    diag_vals = jnp.diagonal(block)
    eye_small = jnp.eye(order, dtype=jnp.float32)
    nilpotent = -jnp.triu(block, 1) / diag_vals[:, None]
    product = eye_small + nilpotent
    power = 2
    while power < order:
        nilpotent = matmul(nilpotent, nilpotent)
        product = matmul(product, eye_small + nilpotent)
        power = power * 2
    return product / diag_vals[None, :]


def tri_inverse(triangle):
    order = triangle.shape[-1]
    count = order // BLOCK
    inverses = [
        small_inverse(triangle[k * BLOCK : (k + 1) * BLOCK, k * BLOCK : (k + 1) * BLOCK])
        for k in range(count)
    ]
    span = BLOCK
    while len(inverses) > 1:
        joined = []
        for pair in range(len(inverses) // 2):
            start = pair * 2 * span
            upper_inv = inverses[2 * pair]
            lower_inv = inverses[2 * pair + 1]
            corner = triangle[start : start + span, start + span : start + 2 * span]
            linked = -matmul(matmul(upper_inv, corner), lower_inv)
            top_rows = jnp.concatenate([upper_inv, linked], axis=1)
            bottom_rows = jnp.concatenate([jnp.zeros_like(lower_inv), lower_inv], axis=1)
            joined.append(jnp.concatenate([top_rows, bottom_rows], axis=0))
        inverses = joined
        span = span * 2
    return inverses[0]


def right_solve(triangle, values):
    return matmul(values, tri_inverse(triangle).T)


def bit_groups(bit_count):
    groups = []
    first_bit = 0
    while first_bit < bit_count:
        span_bits = min(2, bit_count - first_bit)
        groups.append((first_bit, span_bits))
        first_bit = first_bit + span_bits
    return groups


def on_device(leaf_q, q_cot, leaf_tri, node_blocks, node_tri, root_cot):
    bit_count = lax.axis_size("inner").bit_length() - 1
    groups = bit_groups(bit_count)
    levels_count = len(groups) + 1
    blocks_all = node_blocks.astype(jnp.float32)
    tris_all = node_tri.astype(jnp.float32)
    leaf_sums = inner_product(leaf_q, q_cot)
    child_sums = [leaf_sums]
    current = leaf_sums
    for height in range(levels_count - 1):
        first_bit, span_bits = groups[height]
        current = inner_product(blocks_all[height], current)
        for bit_index in range(first_bit, first_bit + span_bits):
            current = current + partner(current, "inner", bit_index)
        child_sums.append(current)
    top_part = inner_product(blocks_all[levels_count - 1], current)
    top_sum = lax.psum(top_part, "outer")
    upper_path = None
    cot_tri = root_cot
    for height in reversed(range(levels_count)):
        node_sum = top_sum if height == levels_count - 1 else child_sums[height + 1]
        own_sum = child_sums[height]
        own_block = blocks_all[height]
        node_triangle = tris_all[height]
        if upper_path is None:
            middle = matmul(node_triangle, cot_tri.T) - node_sum.T
            right_side = own_sum + matmul(own_block, mirror_lower(middle))
            upper_path = own_block
        else:
            middle = matmul(node_triangle, cot_tri.T) - matmul(upper_path, node_sum.T)
            right_side = matmul(own_sum, upper_path.T) + matmul(own_block, mirror_lower(middle))
            upper_path = matmul(own_block, upper_path)
        cot_tri = right_solve(node_triangle, right_side)
    leaf_cot = matmul(q_cot, upper_path.T)
    middle = matmul(leaf_tri, cot_tri.T) - matmul(upper_path, leaf_sums.T)
    return right_solve(leaf_tri, leaf_cot + matmul(leaf_q, mirror_lower(middle)))


def solution(mesh):
    return jax.shard_map(
        on_device,
        mesh=mesh,
        in_specs=(
            P(("outer", "inner"), None),
            P(("outer", "inner"), None),
            P(("outer", "inner"), None),
            P(None, ("outer", "inner"), None),
            P(None, ("outer", "inner"), None),
            P(),
        ),
        out_specs=P(("outer", "inner"), None),
        check_vma=False,
    )
```

profile of v0, /device:TPU:0, one launch (start us, length us, event | category | flops | bytes accessed | tf_op | source)
XLA Modules:
  0.0 120.0 jit_solution(4308424326360771301)
XLA Ops:
  6.5 0.9 copy-done
  7.4 1.3 %fusion.268 = f32[128,128]{1,0:T(8,128)S(1)} fusion(f32[256,128]{1,0:T(8,128)} %param.6, f32[256,128]{1,0:T(8,128)S(1)} %copy-done), kind=kOutput, calls=%fused_computation.439 | convolution fusion | flops 50331648 | bytes 327680 | tf_op jit(solution)/shard_map/dot_general | solution.py:22
  9.0 3.0 %collective-permute-start = (f32[128,128]{0,1:T(8,128)S(1)}, f32[128,128]{0,1:T(8,128)S(1)}, u32[]{:S(2)}, u32[]{:S(2)}) collective-permute-start(f32[128,128]{0,1:T(8,128)S(1)} %convolution_bitcast_fusion.5), channel_id=1, source_target_pairs={{0,1},{1,0},{2,3},{3,2},{4,5},{5,4},{6,7},{7,6},{8,9},{9,8},{10,11... | collective-permute-start | bytes 196616 | tf_op jit(solution)/shard_map/ppermute | solution.py:12
  14.8 1.0 fusion.217
  15.8 0.9 fusion.148
  16.9 0.7 gather_fusion.10
  17.6 1.0 fusion.218
  18.6 0.9 fusion.151
  19.7 0.7 gather_fusion.11
  20.4 1.0 fusion.219
  21.4 0.9 fusion.154
  23.2 1.0 fusion.212
  24.2 0.9 fusion.133
  25.3 0.7 gather_fusion.5
  26.1 1.0 fusion.213
  27.1 0.9 fusion.136
  28.1 0.7 gather_fusion.6
  28.9 1.0 fusion.214
  29.9 0.9 fusion.139
  31.0 0.7 gather_fusion.7
  31.7 1.0 fusion.215
  32.7 0.9 fusion.142
  36.5 0.7 gather_fusion.2
  37.8 0.7 gather_fusion.3
  64.1 1.6 %collective-permute-start.1 = (f32[128,128]{0,1:T(8,128)S(1)}, f32[128,128]{0,1:T(8,128)S(1)}, u32[]{:S(2)}, u32[]{:S(2)}) collective-permute-start(f32[128,128]{0,1:T(8,128)S(1)} %add.355), channel_id=1, source_target_pairs={{0,2},{1,3},{2,0},{3,1},{4,6},{5,7},{6,4},{7,5},{8,10},{9,11},{10,... | collective-permute-start | bytes 196616 | tf_op jit(solution)/shard_map/ppermute | solution.py:12
  66.1 2.3 %collective-permute-done.1 = f32[128,128]{0,1:T(8,128)S(1)} collective-permute-done((f32[128,128]{0,1:T(8,128)S(1)}, f32[128,128]{0,1:T(8,128)S(1)}, u32[]{:S(2)}, u32[]{:S(2)}) %collective-permute-start.1) | collective-permute-done | bytes 65568 | tf_op jit(solution)/shard_map/ppermute | solution.py:12
  68.7 2.6 %collective-permute-start.2 = (f32[128,128]{0,1:T(8,128)S(1)}, f32[128,128]{0,1:T(8,128)S(1)}, u32[]{:S(2)}, u32[]{:S(2)}) collective-permute-start(f32[128,128]{0,1:T(8,128)S(1)} %convolution_bitcast_fusion.4), channel_id=1, source_target_pairs={{0,4},{1,5},{2,6},{3,7},{4,0},{5,1},{6,2},{7,3},{8,12},{9,13},{10,... | collective-permute-start | bytes 196616 | tf_op jit(solution)/shard_map/ppermute | solution.py:12
  71.3 2.6 %collective-permute-done.2 = f32[128,128]{0,1:T(8,128)S(1)} collective-permute-done((f32[128,128]{0,1:T(8,128)S(1)}, f32[128,128]{0,1:T(8,128)S(1)}, u32[]{:S(2)}, u32[]{:S(2)}) %collective-permute-start.2) | collective-permute-done | bytes 65568 | tf_op jit(solution)/shard_map/ppermute | solution.py:12
  73.9 0.9 convolution_bitcast_fusion.3
  75.1 31.8 %all-reduce.14.cloned.1.call-done = f32[128,128]{1,0:T(8,128)} async-done(((f32[128,128]{1,0:T(8,128)}), f32[128,128]{1,0:T(8,128)}) %all-reduce.14.cloned.1.call-update) | async-done | bytes 65552 | tf_op jit(solution)/shard_map/psum | solution.py:103
  106.8 1.0 copy.17
  112.1 1.1 fusion.2
  (212 shorter events, 37.8 us)
Async XLA Ops:
  6.5 0.9 copy-start
  6.5 2.2 %copy-start.1 = (bf16[3,128,128]{2,1,0:T(8,128)(2,1)S(1)}, bf16[3,128,128]{2,1,0:T(8,128)(2,1)}, u32[]{:S(2)}) copy-start(bf16[3,128,128]{2,1,0:T(8,128)(2,1)} %param.9) | copy-start | bytes 294916
  6.5 100.3 %all-reduce.14.cloned.1.call-start = ((), (), s32[]{:S(2)}) async-start(), calls=%async_computation | async-start | bytes 131072 | tf_op jit(solution)/shard_map/psum | solution.py:103
  8.7 3.3 %copy-start.2 = (bf16[3,128,128]{2,1,0:T(8,128)(2,1)S(1)}, bf16[3,128,128]{2,1,0:T(8,128)(2,1)}, u32[]{:S(2)}) copy-start(bf16[3,128,128]{2,1,0:T(8,128)(2,1)} %param.10) | copy-start | bytes 294916
  9.0 55.1 %collective-permute-start = (f32[128,128]{0,1:T(8,128)S(1)}, f32[128,128]{0,1:T(8,128)S(1)}, u32[]{:S(2)}, u32[]{:S(2)}) collective-permute-start(f32[128,128]{0,1:T(8,128)S(1)} %convolution_bitcast_fusion.5), channel_id=1, source_target_pairs={{0,1},{1,0},{2,3},{3,2},{4,5},{5,4},{6,7},{7,6},{8,9},{9,8},{10,11... | collective-permute-start | bytes 196616 | tf_op jit(solution)/shard_map/ppermute | solution.py:12
  12.1 0.6 copy-start.6
  12.1 1.6 %copy-start.7 = (f32[128,128]{1,0:T(8,128)}, f32[128,128]{1,0:T(8,128)S(1)}, u32[]{:S(2)}) copy-start(f32[128,128]{1,0:T(8,128)S(1)} %get-tuple-element.5) | copy-start | bytes 196612
  40.1 0.8 copy-start.3
  57.7 0.8 copy-start.8
  64.1 4.3 %collective-permute-start.1 = (f32[128,128]{0,1:T(8,128)S(1)}, f32[128,128]{0,1:T(8,128)S(1)}, u32[]{:S(2)}, u32[]{:S(2)}) collective-permute-start(f32[128,128]{0,1:T(8,128)S(1)} %add.355), channel_id=1, source_target_pairs={{0,2},{1,3},{2,0},{3,1},{4,6},{5,7},{6,4},{7,5},{8,10},{9,11},{10,... | collective-permute-start | bytes 196616 | tf_op jit(solution)/shard_map/ppermute | solution.py:12
  68.7 5.2 %collective-permute-start.2 = (f32[128,128]{0,1:T(8,128)S(1)}, f32[128,128]{0,1:T(8,128)S(1)}, u32[]{:S(2)}, u32[]{:S(2)}) collective-permute-start(f32[128,128]{0,1:T(8,128)S(1)} %convolution_bitcast_fusion.4), channel_id=1, source_target_pairs={{0,4},{1,5},{2,6},{3,7},{4,0},{5,1},{6,2},{7,3},{8,12},{9,13},{10,... | collective-permute-start | bytes 196616 | tf_op jit(solution)/shard_map/ppermute | solution.py:12
  106.8 1.0 copy-start.5
  110.9 0.9 copy-start.4
Sparse Core Ops, SparseCore 0:
  74.9 31.8 all-reduce.13
where the time goes:
time: 122 us; the launch traced here: 120 us
  matrix products  44.3 us (36%)
  waiting for transfers between devices  36.7 us (30%)
  local copies, waits for them, and re-layouts  17 us (14%)
  between operations  14.4 us (12%)
  starting transfers between devices  7.32 us (6%)
    dot_general x172, matrix products, matmul(): jnp.dot(left_side, right_side, precision=lax.Precision.HIGHEST, preferred...  41.7 us
    psum x1, waiting for transfers between devices, on_device(): top_sum = lax.psum(top_part, 'outer')  31.8 us
    gather x16, local copies, waits for them, and re-layouts, small_inverse(): diag_vals = jnp.diagonal(block)  11.7 us
    ppermute x3, starting transfers between devices, partner(): return lax.ppermute(value, axis, pairs)  7.32 us
    ppermute x3, waiting for transfers between devices, partner(): return lax.ppermute(value, axis, pairs)  4.9 us
    unnamed x18, local copies, waits for them, and re-layouts  3.11 us
    dot_general x4, matrix products, inner_product(): lax.dot_general(left_side, right_side, (((0,), (0,)), ((), ())), precisio...  2.57 us
  transfers between devices with their start and end apart: 4, of which 3 were waited for; matrix products, arithmetic and copies ran while one was open for 42% of the time, Pallas kernels for 0%

commit v1 on v0

v1 whole, which is shorter than its diff:
```python
import functools

import jax
import jax.numpy as jnp
from jax import lax
from jax.experimental import pallas as pl
from jax.experimental.pallas import tpu as pltpu
from jax.sharding import PartitionSpec as P

BLOCK = 32
MESH = pl.DeviceIdType.MESH
F32 = jnp.float32
BF16 = jnp.bfloat16


def split(value):
    high = value.astype(BF16)
    return high, (value - high.astype(F32)).astype(BF16)


def dot(left, right, dims):
    return lax.dot_general(left, right, (dims, ((), ())), preferred_element_type=F32)


def product(left, right, dims=((1,), (0,))):
    left_high, left_low = left
    right_high, right_low = right
    total = dot(left_high, right_high, dims)
    if right_low is not None:
        total = total + dot(left_high, right_low, dims)
    if left_low is not None:
        total = total + dot(left_low, right_high, dims)
    return total


def places(order):
    rows = lax.broadcasted_iota(jnp.int32, (order, order), 0)
    columns = lax.broadcasted_iota(jnp.int32, (order, order), 1)
    return rows, columns


def mirror_lower(matrix, rows, columns):
    below = jnp.where(rows > columns, matrix, 0.0)
    return jnp.where(rows >= columns, matrix, 0.0) + below.T


def block_inverses(triangles, rows, columns):
    inside = (rows // BLOCK == columns // BLOCK) & (rows < columns)
    on_diagonal = rows == columns
    eye = jnp.where(on_diagonal, 1.0, 0.0)
    powers, totals, scales = [], [], []
    for triangle in triangles:
        diagonal = jnp.where(on_diagonal, triangle, 0.0)
        down = jnp.sum(diagonal, axis=1, keepdims=True)
        scales.append(jnp.sum(diagonal, axis=0, keepdims=True))
        nilpotent = jnp.where(inside, -triangle, 0.0) / down
        powers.append(split(nilpotent))
        totals.append(eye + nilpotent)
    power = 2
    while power < BLOCK:
        powers = [split(product(value, value)) for value in powers]
        totals = [total + product(split(total), value) for total, value in zip(totals, powers)]
        power = power * 2
    return [total / scale for total, scale in zip(totals, scales)]


def join_inverses(inverses, triangles, rows, columns):
    order = rows.shape[0]
    span = BLOCK
    while span < order:
        corner = (rows // (2 * span) == columns // (2 * span)) & (rows // span < columns // span)
        joined = []
        for inverse, triangle in zip(inverses, triangles):
            parts = split(inverse)
            link = product(parts, split(jnp.where(corner, triangle, 0.0)))
            joined.append(inverse - product(split(link), parts))
        inverses = joined
        span = span * 2
    return inverses


def fan_list(n_outer, n_inner):
    fanins = []
    remain = n_inner
    while remain > 1:
        fanins.append(min(remain, 4))
        remain = remain // fanins[-1]
    fanins.append(n_outer)
    return fanins


def kernel(
    n_outer, n_inner,
    q_hbm, g_hbm, leaf_hbm, blocks_hbm, tri_hbm, root_hbm, out_ref,
    q_ref, g_ref, leaf_ref, blocks_ref, tri_ref, root_ref,
    part_ref, scatter_ref, lift_ref, land_ref, full_ref,
    in_sem, scatter_send, scatter_recv, lift_send, lift_recv, full_send, full_recv,
):
    fanins = fan_list(n_outer, n_inner)
    levels = len(fanins)
    outer, inner = lax.axis_index("outer"), lax.axis_index("inner")
    order = leaf_ref.shape[1]
    first = fanins[0]
    chunk = order // first

    def digit(level):
        if level == levels - 1:
            return outer
        stride = 1
        for factor in fanins[:level]:
            stride = stride * factor
        return lax.rem(inner // stride, fanins[level])

    def peer(level, step):
        mine = digit(level)
        other = lax.rem(mine + step, fanins[level])
        if level == levels - 1:
            return other, (other, inner)
        stride = 1
        for factor in fanins[:level]:
            stride = stride * factor
        return other, (outer, inner + (other - mine) * stride)

    loads = [
        pltpu.make_async_copy(source, target, in_sem.at[k])
        for k, (source, target) in enumerate(
            [
                (g_hbm, g_ref), (q_hbm, q_ref), (blocks_hbm, blocks_ref),
                (leaf_hbm, leaf_ref), (tri_hbm, tri_ref), (root_hbm, root_ref),
            ]
        )
    ]
    for load in loads:
        load.start()
    barrier = pltpu.get_barrier_semaphore()
    greeted = 0
    for level in range(levels):
        for step in range(1, fanins[level]):
            pl.semaphore_signal(barrier, inc=1, device_id=peer(level, step)[1], device_id_type=MESH)
            greeted += 1

    rows, columns = places(order)
    for load in loads[:3]:
        load.wait()
    blocks = [blocks_ref[level] for level in range(levels)]
    cot_parts = split(g_ref[...])
    row_parts = split(q_ref[...])
    leaf_sum = product(split(g_ref[...].T), row_parts)
    leaf_parts = split(leaf_sum)
    part_ref[...] = product(leaf_parts, (blocks[0], None))
    pl.semaphore_wait(barrier, greeted)

    mine = digit(0)
    own = pl.ds(pl.multiple_of(mine * chunk, chunk), chunk)
    scatters = []
    for step in range(1, first):
        other, device = peer(0, step)
        copy = pltpu.make_async_remote_copy(
            src_ref=part_ref.at[pl.ds(pl.multiple_of(other * chunk, chunk), chunk)],
            dst_ref=scatter_ref.at[step - 1],
            send_sem=scatter_send.at[step - 1],
            recv_sem=scatter_recv.at[step - 1],
            device_id=device,
            device_id_type=MESH,
        )
        copy.start()
        scatters.append(copy)

    def spread(level):
        copies = []
        for step in range(1, first):
            copy = pltpu.make_async_remote_copy(
                src_ref=full_ref.at[level, own],
                dst_ref=full_ref.at[level, own],
                send_sem=full_send.at[level, step - 1],
                recv_sem=full_recv.at[level, step - 1],
                device_id=peer(0, step)[1],
                device_id_type=MESH,
            )
            copy.start()
            copies.append(copy)
        return copies

    def lift(level):
        copies = []
        for step in range(1, fanins[level]):
            copy = pltpu.make_async_remote_copy(
                src_ref=lift_ref.at[level - 1],
                dst_ref=land_ref.at[level - 1, step - 1],
                send_sem=lift_send.at[level - 1, step - 1],
                recv_sem=lift_recv.at[level - 1, step - 1],
                device_id=peer(level, step)[1],
                device_id_type=MESH,
            )
            copy.start()
            copies.append(copy)
        return copies

    for load in loads[3:]:
        load.wait()
    triangles = [leaf_ref[...]] + [tri_ref[level].astype(F32) for level in range(levels)]
    inverses = block_inverses(triangles, rows, columns)

    for copy in scatters:
        copy.wait_recv()
    total = part_ref[own, :]
    for step in range(1, first):
        total = total + scatter_ref[step - 1]
    full_ref[0, own, :] = total

    spreads, lifts = [], []
    late = {}

    def paths_and_inverses():
        late["inverses"] = [split(x) for x in join_inverses(inverses, triangles, rows, columns)]
        path = [None] * levels
        path[levels - 1] = (blocks[levels - 1], None)
        for level in reversed(range(levels - 1)):
            path[level] = split(product((blocks[level], None), path[level + 1]))
        late["path"] = path

    def carries():
        inv, path = late["inverses"], late["path"]
        tri_parts = [split(triangles[0])] + [(tri_ref[level], None) for level in range(levels - 1)]
        ratio = [split(product(tri_parts[level], inv[level + 1])) for level in range(levels)]
        late["ratio"] = ratio
        weight = []
        for level in range(levels):
            through = path[level][0].astype(F32)
            if path[level][1] is not None:
                through = through + path[level][1].astype(F32)
            if level == levels - 1:
                carried = ratio[level][0].astype(F32) + ratio[level][1].astype(F32)
            else:
                carried = product(ratio[level], path[level + 1])
            weight.append(split(carried - through))
        late["weight"] = weight
        late["below"] = product(weight[0], leaf_parts)
        late["cot"] = product(
            cot_parts, split(product(inv[0], path[0])), ((1,), (1,))
        )
        late["top"] = product((tri_ref[levels - 1], None), split(root_ref[...]), ((1,), (1,)))

    work = {1: paths_and_inverses, levels - 1: carries}
    done = set()
    for level in range(1, levels):
        lift_ref[level - 1] = product(split(total), (blocks[level], None))
        lifts.append(lift(level))
        spreads.append(spread(level - 1))
        if level == 1:
            paths_and_inverses()
        if level == levels - 1:
            carries()
        for copy in lifts[-1]:
            copy.wait_recv()
        total = lift_ref[level - 1]
        for step in range(1, fanins[level]):
            total = total + land_ref[level - 1, step - 1]
        full_ref[level, own, :] = total
    spreads.append(spread(levels - 1))

    known = [late["below"]]
    for level in range(levels - 1):
        for copy in spreads[level]:
            copy.wait_recv()
        known.append(product(late["weight"][level + 1], split(full_ref[level])))

    for copy in spreads[levels - 1]:
        copy.wait_recv()
    middle = late["top"] - full_ref[levels - 1]
    for level in reversed(range(levels)):
        mirrored = split(mirror_lower(middle, rows, columns))
        turned = product(mirrored, (blocks[level], None), ((1,), (1,)))
        middle = known[level] + product(late["ratio"][level], split(turned))
    mirrored = split(mirror_lower(middle, rows, columns))
    solved = split(product(mirrored, late["inverses"][0], ((1,), (1,))))
    out_ref[...] = late["cot"] + product(row_parts, solved)

    for copy in scatters:
        copy.wait_send()
    for copies in lifts + spreads:
        for copy in copies:
            copy.wait_send()


def on_device(n_outer, n_inner, leaf_q, q_cot, leaf_tri, node_blocks, node_tri, root_cot):
    fanins = fan_list(n_outer, n_inner)
    levels = len(fanins)
    order = leaf_tri.shape[1]
    chunk = order // fanins[0]
    widest = max(fanins[1:])
    dma = pltpu.SemaphoreType.DMA
    args = (leaf_q, q_cot, leaf_tri, node_blocks, node_tri, root_cot)
    return pl.pallas_call(
        functools.partial(kernel, n_outer, n_inner),
        out_shape=jax.ShapeDtypeStruct(leaf_q.shape, F32),
        in_specs=[pl.BlockSpec(memory_space=pl.ANY)] * len(args),
        out_specs=pl.BlockSpec(memory_space=pltpu.VMEM),
        scratch_shapes=[pltpu.VMEM(arg.shape, arg.dtype) for arg in args]
        + [
            pltpu.VMEM((order, order), F32),
            pltpu.VMEM((fanins[0] - 1, chunk, order), F32),
            pltpu.VMEM((levels - 1, chunk, order), F32),
            pltpu.VMEM((levels - 1, widest - 1, chunk, order), F32),
            pltpu.VMEM((levels, order, order), F32),
            dma((len(args),)),
            dma((fanins[0] - 1,)),
            dma((fanins[0] - 1,)),
            dma((levels - 1, widest - 1)),
            dma((levels - 1, widest - 1)),
            dma((levels, fanins[0] - 1)),
            dma((levels, fanins[0] - 1)),
        ],
        compiler_params=pltpu.CompilerParams(
            collective_id=0, has_side_effects=True, vmem_limit_bytes=32 * 2**20
        ),
    )(*args)


def solution(mesh):
    return jax.shard_map(
        functools.partial(on_device, mesh.shape["outer"], mesh.shape["inner"]),
        mesh=mesh,
        in_specs=(
            P(("outer", "inner"), None),
            P(("outer", "inner"), None),
            P(("outer", "inner"), None),
            P(None, ("outer", "inner"), None),
            P(None, ("outer", "inner"), None),
            P(),
        ),
        out_specs=P(("outer", "inner"), None),
        check_vma=False,
    )
```

time: 122 us -> 28 us (0.23); the launches traced: 120 us -> 27.7 us
  matrix products: 44.3 us -> 0 us
  waiting for transfers between devices: 36.7 us -> 0 us
  Pallas kernels: 0 us -> 21.8 us
  between operations: 14.4 us -> 0.02 us
  local copies, waits for them, and re-layouts: 17 us -> 5.93 us
  starting transfers between devices: 7.32 us -> 0 us
    dot_general x176 -> x0, matrix products: 44.3 us -> none  [the longest x172 41.7 us: matmul(): jnp.dot(left_side, right_side, precision=lax.Precision.HIGHEST, preferred...]
    psum x1 -> x0, waiting for transfers between devices: 31.8 us -> none  [on_device(): top_sum = lax.psum(top_part, 'outer')]
    pallas_call x0 -> x1, Pallas kernels: none -> 21.8 us  [on_device(): pl.pallas_call(functools.partial(kernel, n_outer, n_inner), out_shape=jax...]
    gather x16 -> x0, local copies, waits for them, and re-layouts: 11.7 us -> none  [small_inverse(): diag_vals = jnp.diagonal(block)]
    ppermute x3 -> x0, starting transfers between devices: 7.32 us -> none  [partner(): return lax.ppermute(value, axis, pairs)]
    ppermute x3 -> x0, waiting for transfers between devices: 4.9 us -> none  [partner(): return lax.ppermute(value, axis, pairs)]
    unnamed x18 -> x13, local copies, waits for them, and re-layouts: 3.11 us -> 5.93 us
  transfers between devices with their start and end apart: 4 -> 0, of which waited for: 3 -> 0; matrix products, arithmetic and copies ran while one was open for 42% -> 0% of each run, Pallas kernels for 0% -> 0%
where the time goes in v1:
time: 28 us; the launch traced here: 27.7 us
  Pallas kernels  21.8 us (78%)
  local copies, waits for them, and re-layouts  5.93 us (21%)
    pallas_call x1, Pallas kernels, on_device(): pl.pallas_call(functools.partial(kernel, n_outer, n_inner), out_shape=jax...  21.8 us
    unnamed x13, local copies, waits for them, and re-layouts  5.93 us

profile of v1, /device:TPU:0, one launch (start us, length us, event | category | flops | bytes accessed | tf_op | source)
XLA Modules:
  0.0 27.7 jit_solution(11276237277277154842)
XLA Ops:
  0.0 0.0 copy-start
  0.0 0.9 %copy-done = f32[256,128]{1,0:T(8,128)S(1)} copy-done((f32[256,128]{1,0:T(8,128)S(1)}, f32[256,128]{1,0:T(8,128)}, u32[]{:S(2)}) %copy-start) | copy-done | bytes 131096
  0.9 0.0 copy-start.1
  0.9 0.9 %copy-done.1 = f32[256,128]{1,0:T(8,128)S(1)} copy-done((f32[256,128]{1,0:T(8,128)S(1)}, f32[256,128]{1,0:T(8,128)}, u32[]{:S(2)}) %copy-start.1) | copy-done | bytes 131096
  1.8 0.0 copy-start.2
  1.8 0.9 %copy-done.2 = bf16[3,128,128]{2,1,0:T(8,128)(2,1)S(1)} copy-done((bf16[3,128,128]{2,1,0:T(8,128)(2,1)S(1)}, bf16[3,128,128]{2,1,0:T(8,128)(2,1)}, u32[]{:S(2)}) %copy-start.2) | copy-done | bytes 98328
  2.7 0.0 copy-start.3
  2.7 0.9 %copy-done.3 = bf16[3,128,128]{2,1,0:T(8,128)(2,1)S(1)} copy-done((bf16[3,128,128]{2,1,0:T(8,128)(2,1)S(1)}, bf16[3,128,128]{2,1,0:T(8,128)(2,1)}, u32[]{:S(2)}) %copy-start.3) | copy-done | bytes 98328
  3.6 0.0 copy-start.4
  3.6 0.8 %copy-done.4 = f32[128,128]{1,0:T(8,128)S(1)} copy-done((f32[128,128]{1,0:T(8,128)S(1)}, f32[128,128]{1,0:T(8,128)}, u32[]{:S(2)}) %copy-start.4) | copy-done | bytes 65560
  4.4 0.0 copy-start.5
  4.4 0.8 %copy-done.5 = f32[128,128]{1,0:T(8,128)S(1)} copy-done((f32[128,128]{1,0:T(8,128)S(1)}, f32[128,128]{1,0:T(8,128)}, u32[]{:S(2)}) %copy-start.5) | copy-done | bytes 65560
  5.3 21.8 %shard_map.64 = f32[256,128]{1,0:T(8,128)S(1)} custom-call(f32[256,128]{1,0:T(8,128)S(1)} %copy-done, f32[256,128]{1,0:T(8,128)S(1)} %copy-done.1, f32[128,128]{1,0:T(8,128)S(1)} %copy-done.4, bf16[3,128,128]{2,1,0:T(8,128)(2,1)S(1)} %copy-done.2, bf16[3,128,128]{2,1,0:T(8,128)(2,1)S(1)} %copy-done.3, f32[128,128]{1,0:T(8,128)S(1)} %copy-done.5), custom_call_target="tpu_custom_call" | custom-call | tf_op jit(solution)/shard_map/pallas_call | solution.py:294
  27.0 0.7 %copy.8 = f32[256,128]{1,0:T(8,128)} copy(f32[256,128]{1,0:T(8,128)S(1)} %shard_map.64) | data formatting | bytes 262144
Async XLA Ops:
  0.0 0.9 %copy-start = (f32[256,128]{1,0:T(8,128)S(1)}, f32[256,128]{1,0:T(8,128)}, u32[]{:S(2)}) copy-start(f32[256,128]{1,0:T(8,128)} %q_hbm.1) | copy-start | bytes 393220
  0.9 0.9 %copy-start.1 = (f32[256,128]{1,0:T(8,128)S(1)}, f32[256,128]{1,0:T(8,128)}, u32[]{:S(2)}) copy-start(f32[256,128]{1,0:T(8,128)} %g_hbm.1) | copy-start | bytes 393220
  1.8 0.9 %copy-start.2 = (bf16[3,128,128]{2,1,0:T(8,128)(2,1)S(1)}, bf16[3,128,128]{2,1,0:T(8,128)(2,1)}, u32[]{:S(2)}) copy-start(bf16[3,128,128]{2,1,0:T(8,128)(2,1)} %blocks_hbm.1) | copy-start | bytes 294916
  2.7 0.9 %copy-start.3 = (bf16[3,128,128]{2,1,0:T(8,128)(2,1)S(1)}, bf16[3,128,128]{2,1,0:T(8,128)(2,1)}, u32[]{:S(2)}) copy-start(bf16[3,128,128]{2,1,0:T(8,128)(2,1)} %tri_hbm.1) | copy-start | bytes 294916
  3.6 0.8 %copy-start.4 = (f32[128,128]{1,0:T(8,128)S(1)}, f32[128,128]{1,0:T(8,128)}, u32[]{:S(2)}) copy-start(f32[128,128]{1,0:T(8,128)} %leaf_hbm.1) | copy-start | bytes 196612
  4.4 0.8 %copy-start.5 = (f32[128,128]{1,0:T(8,128)S(1)}, f32[128,128]{1,0:T(8,128)}, u32[]{:S(2)}) copy-start(f32[128,128]{1,0:T(8,128)} %root_hbm.1) | copy-start | bytes 196612

commit v2 on v1

--- a/solution.py
+++ b/solution.py
@@ -18,18 +18,22 @@
     return high, (value - high.astype(F32)).astype(BF16)
 
 
-def dot(left, right, dims):
-    return lax.dot_general(left, right, (dims, ((), ())), preferred_element_type=F32)
-
-
-def product(left, right, dims=((1,), (0,))):
+def product(left, right, turn_right=False):
     left_high, left_low = left
     right_high, right_low = right
-    total = dot(left_high, right_high, dims)
+    width = right_high.shape[0 if turn_right else 1]
+    along, across = (1, 0) if turn_right else (0, 1)
+    wide = right_high
     if right_low is not None:
-        total = total + dot(left_high, right_low, dims)
+        wide = jnp.concatenate([right_high, right_low], axis=across)
     if left_low is not None:
-        total = total + dot(left_low, right_high, dims)
+        wide = jnp.concatenate([wide, wide], axis=along)
+        left_high = jnp.concatenate([left_high, left_low], axis=1)
+    total = lax.dot_general(
+        left_high, wide, (((1,), (along,)), ((), ())), preferred_element_type=F32
+    )
+    if right_low is not None:
+        total = total[:, :width] + total[:, width:]
     return total
 
 
@@ -48,19 +52,28 @@
     inside = (rows // BLOCK == columns // BLOCK) & (rows < columns)
     on_diagonal = rows == columns
     eye = jnp.where(on_diagonal, 1.0, 0.0)
-    powers, totals, scales = [], [], []
+    order = rows.shape[0]
+    stacks, scales = [], []
     for triangle in triangles:
         diagonal = jnp.where(on_diagonal, triangle, 0.0)
         down = jnp.sum(diagonal, axis=1, keepdims=True)
         scales.append(jnp.sum(diagonal, axis=0, keepdims=True))
         nilpotent = jnp.where(inside, -triangle, 0.0) / down
-        powers.append(split(nilpotent))
-        totals.append(eye + nilpotent)
+        stacks.append((nilpotent, eye + nilpotent))
     power = 2
     while power < BLOCK:
-        powers = [split(product(value, value)) for value in powers]
-        totals = [total + product(split(total), value) for total, value in zip(totals, powers)]
+        following = []
+        for nilpotent, total in stacks:
+            parts = split(nilpotent)
+            if power == 2:
+                square = product(parts, parts)
+                following.append((square, total))
+                continue
+            both = product(split(jnp.concatenate([nilpotent, total], axis=0)), parts)
+            following.append((both[:order], total + both[order:]))
+        stacks = following
         power = power * 2
+    totals = [total + product(split(total), split(nilpotent)) for nilpotent, total in stacks]
     return [total / scale for total, scale in zip(totals, scales)]
 
 
@@ -236,13 +249,9 @@
             weight.append(split(carried - through))
         late["weight"] = weight
         late["below"] = product(weight[0], leaf_parts)
-        late["cot"] = product(
-            cot_parts, split(product(inv[0], path[0])), ((1,), (1,))
-        )
-        late["top"] = product((tri_ref[levels - 1], None), split(root_ref[...]), ((1,), (1,)))
-
-    work = {1: paths_and_inverses, levels - 1: carries}
-    done = set()
+        late["cot"] = product(cot_parts, split(product(inv[0], path[0])), True)
+        late["top"] = product((tri_ref[levels - 1], None), split(root_ref[...]), True)
+
     for level in range(1, levels):
         lift_ref[level - 1] = product(split(total), (blocks[level], None))
         lifts.append(lift(level))
@@ -270,10 +279,10 @@
     middle = late["top"] - full_ref[levels - 1]
     for level in reversed(range(levels)):
         mirrored = split(mirror_lower(middle, rows, columns))
-        turned = product(mirrored, (blocks[level], None), ((1,), (1,)))
+        turned = product(mirrored, (blocks[level], None), True)
         middle = known[level] + product(late["ratio"][level], split(turned))
     mirrored = split(mirror_lower(middle, rows, columns))
-    solved = split(product(mirrored, late["inverses"][0], ((1,), (1,))))
+    solved = split(product(mirrored, late["inverses"][0], True))
     out_ref[...] = late["cot"] + product(row_parts, solved)
 
     for copy in scatters:
@@ -294,7 +303,7 @@
     return pl.pallas_call(
         functools.partial(kernel, n_outer, n_inner),
         out_shape=jax.ShapeDtypeStruct(leaf_q.shape, F32),
-        in_specs=[pl.BlockSpec(memory_space=pl.ANY)] * len(args),
+        in_specs=[pl.BlockSpec(memory_space=pltpu.HBM)] * len(args),
         out_specs=pl.BlockSpec(memory_space=pltpu.VMEM),
         scratch_shapes=[pltpu.VMEM(arg.shape, arg.dtype) for arg in args]
         + [
@@ -312,7 +321,7 @@
             dma((levels, fanins[0] - 1)),
         ],
         compiler_params=pltpu.CompilerParams(
-            collective_id=0, has_side_effects=True, vmem_limit_bytes=32 * 2**20
+            collective_id=0, has_side_effects=True, vmem_limit_bytes=60 * 2**20
         ),
     )(*args)
 

time: 28 us -> 23.1 us (0.83)
  local copies, waits for them, and re-layouts: 5.93 us -> 1.57 us
  Pallas kernels: 21.8 us -> 21.4 us
    unnamed x13 -> x1, local copies, waits for them, and re-layouts: 5.93 us -> 1.57 us
    pallas_call x1, Pallas kernels: 21.8 us -> 21.4 us  [on_device(): pl.pallas_call(functools.partial(kernel, n_outer, n_inner), out_shape=jax...]
where the time goes in v2:
time: 23.1 us; the launch traced here: 22.9 us
  Pallas kernels  21.4 us (93%)
  local copies, waits for them, and re-layouts  1.57 us (7%)
    pallas_call x1, Pallas kernels, on_device(): pl.pallas_call(functools.partial(kernel, n_outer, n_inner), out_shape=jax...  21.4 us
    unnamed x1, local copies, waits for them, and re-layouts  1.57 us

profile of v2, /device:TPU:0, one launch (start us, length us, event | category | flops | bytes accessed | tf_op | source)
XLA Modules:
  0.0 22.9 jit_solution(11027289440984044836)
XLA Ops:
  0.0 21.4 %shard_map.64 = f32[256,128]{1,0:T(8,128)} custom-call(f32[256,128]{1,0:T(8,128)} %q_hbm.1, f32[256,128]{1,0:T(8,128)} %g_hbm.1, f32[128,128]{1,0:T(8,128)} %leaf_hbm.1, bf16[3,128,128]{2,1,0:T(8,128)(2,1)} %blocks_hbm.1, bf16[3,128,128]{2,1,0:T(8,128)(2,1)} %tri_hbm.1, f32[128,128]{1,0:T(8,128)} %root_hbm.1), custom_call_target="tpu_custom_call" | custom-call | tf_op jit(solution)/shard_map/pallas_call | solution.py:303
  21.4 1.6 %copy.8 = f32[256,128]{1,0:T(8,128)} copy(f32[256,128]{1,0:T(8,128)} %shard_map.64) | data formatting | bytes 262144

commit v3 on v2

v3 whole, which is shorter than its diff:
```python
import functools

import jax
import jax.numpy as jnp
from jax import lax
from jax.experimental import pallas as pl
from jax.experimental.pallas import tpu as pltpu
from jax.sharding import PartitionSpec as P

BLOCK = 32
MESH = pl.DeviceIdType.MESH
F32 = jnp.float32
BF16 = jnp.bfloat16


def split(value):
    high = value.astype(BF16)
    return high, (value - high.astype(F32)).astype(BF16)


def product(left, right, turn_right=False):
    left_high, left_low = left
    right_high, right_low = right
    width = right_high.shape[0 if turn_right else 1]
    along, across = (1, 0) if turn_right else (0, 1)
    wide = right_high
    if right_low is not None:
        wide = jnp.concatenate([right_high, right_low], axis=across)
    if left_low is not None:
        wide = jnp.concatenate([wide, wide], axis=along)
        left_high = jnp.concatenate([left_high, left_low], axis=1)
    total = lax.dot_general(
        left_high, wide, (((1,), (along,)), ((), ())), preferred_element_type=F32
    )
    if right_low is not None:
        total = total[:, :width] + total[:, width:]
    return total


def places(order):
    rows = lax.broadcasted_iota(jnp.int32, (order, order), 0)
    columns = lax.broadcasted_iota(jnp.int32, (order, order), 1)
    return rows, columns


def mirror_lower(matrix, rows, columns):
    below = jnp.where(rows > columns, matrix, 0.0)
    return jnp.where(rows >= columns, matrix, 0.0) + below.T


def unpack(parts, inside):
    copies = inside.shape[0] // parts[0].shape[0]
    return tuple(jnp.concatenate([part] * copies, axis=0) * inside for part in parts)


def fold(matrix, span):
    total = matrix[:span]
    for start in range(span, matrix.shape[0], span):
        total = total + matrix[start : start + span]
    return total


def block_inverses(triangles, rows, columns):
    same = rows // BLOCK == columns // BLOCK
    inside = jnp.where(same, 1.0, 0.0).astype(BF16)
    on_diagonal = rows == columns
    eye = fold(jnp.where(on_diagonal, 1.0, 0.0), BLOCK)
    stacks, scales = [], []
    for triangle in triangles:
        diagonal = jnp.where(on_diagonal, triangle, 0.0)
        down = jnp.sum(diagonal, axis=1, keepdims=True)
        scales.append(jnp.sum(diagonal, axis=0, keepdims=True))
        nilpotent = fold(jnp.where(same & (rows < columns), -triangle, 0.0) / down, BLOCK)
        stacks.append((nilpotent, eye + nilpotent))
    power = 2
    while power < BLOCK:
        following = []
        for nilpotent, total in stacks:
            parts = split(nilpotent)
            if power == 2:
                following.append((product(parts, unpack(parts, inside)), total))
                continue
            stacked = split(jnp.concatenate([nilpotent, total], axis=0))
            both = product(stacked, unpack(parts, inside))
            following.append((both[:BLOCK], total + both[BLOCK:]))
        stacks = following
        power = power * 2
    return [
        (total + product(split(total), unpack(split(nilpotent), inside))) / scale
        for (nilpotent, total), scale in zip(stacks, scales)
    ]


def join_inverses(inverses, triangle_parts, rows, columns):
    order = rows.shape[0]
    span = BLOCK
    while span < order:
        row_block, column_block = rows // span, columns // span
        corner = (rows // (2 * span) == columns // (2 * span)) & (row_block < column_block)
        corner = jnp.where(corner, 1.0, 0.0).astype(BF16)
        inside = jnp.where(row_block == column_block, 1.0, 0.0).astype(BF16)
        even = lax.rem(column_block[:span], 2) == 0
        joined = []
        for inverse, (high, low) in zip(inverses, triangle_parts):
            edge = (high * corner, None if low is None else low * corner)
            upper = split(jnp.where(even, inverse, 0.0))
            link = product(split(product(upper, edge)), unpack(split(inverse), inside))
            top = jnp.where(even, inverse, -link)
            joined.append(jnp.concatenate([top, jnp.where(even, 0.0, inverse)], axis=0))
        inverses = joined
        span = span * 2
    return inverses


def fan_list(n_outer, n_inner):
    fanins = []
    remain = n_inner
    while remain > 1:
        fanins.append(min(remain, 4))
        remain = remain // fanins[-1]
    fanins.append(n_outer)
    return fanins


def scatter_groups(fanins, order):
    groups = [fanins[0]]
    if len(fanins) > 2 and order % (8 * fanins[0] * fanins[1]) == 0:
        groups.append(fanins[0] * fanins[1])
    return groups


def add_all(terms):
    while len(terms) > 1:
        pairs = [left + right for left, right in zip(terms[::2], terms[1::2])]
        terms = pairs + terms[len(terms) & ~1 :]
    return terms[0]


def kernel(
    n_outer, n_inner,
    q_hbm, g_hbm, leaf_hbm, blocks_hbm, tri_hbm, root_hbm, out_ref,
    q_ref, g_ref, leaf_ref, blocks_ref, tri_ref, root_ref,
    part_ref, scatter_ref, lift_ref, land_ref, full_ref,
    in_sem, scatter_send, scatter_recv, lift_send, lift_recv, full_send, full_recv,
):
    fanins = fan_list(n_outer, n_inner)
    levels = len(fanins)
    groups = scatter_groups(fanins, leaf_ref.shape[1])
    merged = len(groups)
    outer, inner = lax.axis_index("outer"), lax.axis_index("inner")
    order = leaf_ref.shape[1]

    def near(size, step):
        mine = lax.rem(inner, size)
        other = lax.rem(mine + step, size)
        return other, (outer, inner + other - mine)

    def above(level, step):
        if level == levels - 1:
            return (lax.rem(outer + step, n_outer), inner)
        stride = 1
        for factor in fanins[:level]:
            stride = stride * factor
        mine = lax.rem(inner // stride, fanins[level])
        other = lax.rem(mine + step, fanins[level])
        return (outer, inner + (other - mine) * stride)

    def own_rows(size):
        rows_each = order // size
        return pl.ds(pl.multiple_of(lax.rem(inner, size) * rows_each, rows_each), rows_each)

    loads = [
        pltpu.make_async_copy(source, target, in_sem.at[k])
        for k, (source, target) in enumerate(
            [
                (g_hbm, g_ref), (q_hbm, q_ref), (blocks_hbm, blocks_ref),
                (leaf_hbm, leaf_ref), (tri_hbm, tri_ref), (root_hbm, root_ref),
            ]
        )
    ]
    for load in loads:
        load.start()
    barrier = pltpu.get_barrier_semaphore()
    greeted = [near(groups[-1], step)[1] for step in range(1, groups[-1])]
    for level in range(merged, levels):
        greeted += [above(level, step) for step in range(1, fanins[level])]
    for device in greeted:
        pl.semaphore_signal(barrier, inc=1, device_id=device, device_id_type=MESH)

    def send(source, target, send_sem, recv_sem, device):
        copy = pltpu.make_async_remote_copy(
            src_ref=source, dst_ref=target, send_sem=send_sem, recv_sem=recv_sem,
            device_id=device, device_id_type=MESH,
        )
        copy.start()
        return copy

    def scatter(level):
        size = groups[level]
        rows_each = order // size
        copies = []
        for step in range(1, size):
            other, device = near(size, step)
            copies.append(
                send(
                    part_ref.at[level, pl.ds(pl.multiple_of(other * rows_each, rows_each), rows_each)],
                    scatter_ref.at[level, step - 1, pl.ds(0, rows_each)],
                    scatter_send.at[level, step - 1], scatter_recv.at[level, step - 1], device,
                )
            )
        return copies

    def gathered(level, copies):
        size = groups[level]
        for copy in copies:
            copy.wait_recv()
        terms = [part_ref[level, own_rows(size), :]]
        terms += [scatter_ref[level, step, : order // size] for step in range(size - 1)]
        return add_all(terms)

    def lift(level, value):
        slot = level - merged
        lift_ref[slot] = value
        return [
            send(
                lift_ref.at[slot], land_ref.at[slot, step - 1],
                lift_send.at[slot, step - 1], lift_recv.at[slot, step - 1], above(level, step),
            )
            for step in range(1, fanins[level])
        ]

    def spread(level, value):
        size = groups[min(level, merged - 1)]
        own = own_rows(size)
        full_ref[level, own, :] = value
        return [
            send(
                full_ref.at[level, own], full_ref.at[level, own],
                full_send.at[level, step - 1], full_recv.at[level, step - 1], near(size, step)[1],
            )
            for step in range(1, size)
        ]

    rows, columns = places(order)
    for load in loads[:3]:
        load.wait()
    blocks = [blocks_ref[level] for level in range(levels)]
    leaf_sum = product(split(g_ref[...].T), split(q_ref[...]))
    leaf_parts = split(leaf_sum)
    climb = (blocks[0], None)
    part_ref[0] = product(leaf_parts, climb)
    for level in range(1, merged):
        climb = split(product(climb, (blocks[level], None)))
        part_ref[level] = product(leaf_parts, climb)
    pl.semaphore_wait(barrier, len(greeted))
    scatters = [None] * merged
    for level in reversed(range(merged)):
        scatters[level] = scatter(level)

    for load in loads[3:]:
        load.wait()
    triangles = [leaf_ref[...]] + [tri_ref[level].astype(F32) for level in range(levels)]
    triangle_parts = [split(triangles[0])] + [(tri_ref[level], None) for level in range(levels)]
    inverses = block_inverses(triangles, rows, columns)

    lifts, spreads = [], [None] * levels
    total = gathered(merged - 1, scatters[merged - 1])
    for level in range(merged, levels):
        value = product(split(total), (blocks[level], None))
        lifts.append(lift(level, value))
        spreads[level - 1] = spread(level - 1, total)
        if level == merged:
            for below in reversed(range(merged - 1)):
                spreads[below] = spread(below, gathered(below, scatters[below]))
            inverse_parts = [
                split(inverse)
                for inverse in join_inverses(inverses, triangle_parts, rows, columns)
            ]
            path = [None] * levels
            path[levels - 1] = (blocks[levels - 1], None)
            for low in reversed(range(levels - 1)):
                path[low] = split(product((blocks[low], None), path[low + 1]))
            ratio_sums = [
                product(triangle_parts[low], inverse_parts[low + 1]) for low in range(levels)
            ]
            ratio = [split(value) for value in ratio_sums]
        for copy in lifts[-1]:
            copy.wait_recv()
        terms = [lift_ref[level - merged]]
        terms += [land_ref[level - merged, step] for step in range(fanins[level] - 1)]
        total = add_all(terms)
    spreads[levels - 1] = spread(levels - 1, total)

    top = product(triangle_parts[levels], split(root_ref[...]), True)
    known = []
    for level in range(levels):
        through = path[level][0].astype(F32)
        if path[level][1] is not None:
            through = through + path[level][1].astype(F32)
        carried = ratio_sums[level]
        if level < levels - 1:
            carried = product(ratio[level], path[level + 1])
        if level == 0:
            own_sums = leaf_parts
        else:
            for copy in spreads[level - 1]:
                copy.wait_recv()
            own_sums = split(full_ref[level - 1])
        known.append(product(split(carried - through), own_sums))
    cot = product(split(g_ref[...]), split(product(inverse_parts[0], path[0])), True)
    row_parts = split(q_ref[...])

    for copy in spreads[levels - 1]:
        copy.wait_recv()
    middle = top - full_ref[levels - 1]
    for level in reversed(range(levels)):
        mirrored = split(mirror_lower(middle, rows, columns))
        turned = product(mirrored, (blocks[level], None), True)
        middle = known[level] + product(ratio[level], split(turned))
    mirrored = split(mirror_lower(middle, rows, columns))
    solved = split(product(mirrored, inverse_parts[0], True))
    out_ref[...] = cot + product(row_parts, solved)

    for copies in scatters + lifts + spreads:
        for copy in copies:
            copy.wait_send()


def on_device(n_outer, n_inner, leaf_q, q_cot, leaf_tri, node_blocks, node_tri, root_cot):
    fanins = fan_list(n_outer, n_inner)
    levels = len(fanins)
    order = leaf_tri.shape[1]
    groups = scatter_groups(fanins, order)
    merged = len(groups)
    lifted = levels - merged
    widest = max(fanins[merged:]) - 1
    near = groups[-1] - 1
    dma = pltpu.SemaphoreType.DMA
    args = (leaf_q, q_cot, leaf_tri, node_blocks, node_tri, root_cot)
    return pl.pallas_call(
        functools.partial(kernel, n_outer, n_inner),
        out_shape=jax.ShapeDtypeStruct(leaf_q.shape, F32),
        in_specs=[pl.BlockSpec(memory_space=pltpu.HBM)] * len(args),
        out_specs=pl.BlockSpec(memory_space=pltpu.VMEM),
        scratch_shapes=[pltpu.VMEM(arg.shape, arg.dtype) for arg in args]
        + [
            pltpu.VMEM((merged, order, order), F32),
            pltpu.VMEM((merged, near, order // groups[0], order), F32),
            pltpu.VMEM((lifted, order // groups[-1], order), F32),
            pltpu.VMEM((lifted, widest, order // groups[-1], order), F32),
            pltpu.VMEM((levels, order, order), F32),
            dma((len(args),)),
            dma((merged, near)),
            dma((merged, near)),
            dma((lifted, widest)),
            dma((lifted, widest)),
            dma((levels, near)),
            dma((levels, near)),
        ],
        compiler_params=pltpu.CompilerParams(
            collective_id=0, has_side_effects=True, vmem_limit_bytes=60 * 2**20
        ),
    )(*args)


def solution(mesh):
    return jax.shard_map(
        functools.partial(on_device, mesh.shape["outer"], mesh.shape["inner"]),
        mesh=mesh,
        in_specs=(
            P(("outer", "inner"), None),
            P(("outer", "inner"), None),
            P(("outer", "inner"), None),
            P(None, ("outer", "inner"), None),
            P(None, ("outer", "inner"), None),
            P(),
        ),
        out_specs=P(("outer", "inner"), None),
        check_vma=False,
    )
```

time: 23.1 us -> 22.4 us (0.970)
  Pallas kernels: 21.4 us -> 20.6 us
    pallas_call x1, Pallas kernels: 21.4 us -> 20.6 us  [on_device(): pl.pallas_call(functools.partial(kernel, n_outer, n_inner), out_shape=jax...]
where the time goes in v3:
time: 22.4 us; the launch traced here: 22.2 us
  Pallas kernels  20.6 us (92%)
  local copies, waits for them, and re-layouts  1.57 us (7%)
    pallas_call x1, Pallas kernels, on_device(): pl.pallas_call(functools.partial(kernel, n_outer, n_inner), out_shape=jax...  20.6 us
    unnamed x1, local copies, waits for them, and re-layouts  1.57 us

profile of v3, /device:TPU:0, one launch (start us, length us, event | category | flops | bytes accessed | tf_op | source)
XLA Modules:
  0.0 22.2 jit_solution(10790463914596003452)
XLA Ops:
  0.0 20.6 %shard_map.64 = f32[256,128]{1,0:T(8,128)} custom-call(f32[256,128]{1,0:T(8,128)} %q_hbm.1, f32[256,128]{1,0:T(8,128)} %g_hbm.1, f32[128,128]{1,0:T(8,128)} %leaf_hbm.1, bf16[3,128,128]{2,1,0:T(8,128)(2,1)} %blocks_hbm.1, bf16[3,128,128]{2,1,0:T(8,128)(2,1)} %tri_hbm.1, f32[128,128]{1,0:T(8,128)} %root_hbm.1), custom_call_target="tpu_custom_call" | custom-call | tf_op jit(solution)/shard_map/pallas_call | solution.py:340
  20.6 1.6 %copy.8 = f32[256,128]{1,0:T(8,128)} copy(f32[256,128]{1,0:T(8,128)} %shard_map.64) | data formatting | bytes 262144

commit v4 on v3

--- a/solution.py
+++ b/solution.py
@@ -358,9 +358,9 @@
             dma((levels, near)),
         ],
         compiler_params=pltpu.CompilerParams(
-            collective_id=0, has_side_effects=True, vmem_limit_bytes=60 * 2**20
+            collective_id=0, has_side_effects=True, vmem_limit_bytes=32 * 2**20
         ),
-    )(*args)
+    )(*[pltpu.with_memory_space_constraint(arg, pltpu.HBM) for arg in args])
 
 
 def solution(mesh):

time: 22.4 us -> 20.8 us (0.929)
  local copies, waits for them, and re-layouts: 1.57 us -> 0.66 us
  Pallas kernels: 20.6 us -> 20 us
    unnamed x1, local copies, waits for them, and re-layouts: 1.57 us -> 0.66 us
    pallas_call x1, Pallas kernels: 20.6 us -> 20 us  [on_device(): pl.pallas_call(functools.partial(kernel, n_outer, n_inner), out_shape=jax...]
where the time goes in v4:
time: 20.8 us; the launch traced here: 20.7 us
  Pallas kernels  20 us (96%)
  local copies, waits for them, and re-layouts  0.66 us (3%)
    pallas_call x1, Pallas kernels, on_device(): pl.pallas_call(functools.partial(kernel, n_outer, n_inner), out_shape=jax...  20 us
    unnamed x1, local copies, waits for them, and re-layouts  0.66 us

profile of v4, /device:TPU:0, one launch (start us, length us, event | category | flops | bytes accessed | tf_op | source)
XLA Modules:
  0.0 20.7 jit_solution(4729518304695665244)
XLA Ops:
  0.0 20.0 %shard_map.64 = f32[256,128]{1,0:T(8,128)S(1)} custom-call(f32[256,128]{1,0:T(8,128)} %q_hbm.1, f32[256,128]{1,0:T(8,128)} %g_hbm.1, f32[128,128]{1,0:T(8,128)} %leaf_hbm.1, bf16[3,128,128]{2,1,0:T(8,128)(2,1)} %blocks_hbm.1, bf16[3,128,128]{2,1,0:T(8,128)(2,1)} %tri_hbm.1, f32[128,128]{1,0:T(8,128)} %root_hbm.1), custom_call_target="tpu_custom_call" | custom-call | tf_op jit(solution)/shard_map/pallas_call | solution.py:340
  20.0 0.7 %copy.8 = f32[256,128]{1,0:T(8,128)} copy(f32[256,128]{1,0:T(8,128)S(1)} %shard_map.64) | data formatting | bytes 262144

commit v5 on v4

--- a/solution.py
+++ b/solution.py
@@ -247,16 +247,21 @@
     blocks = [blocks_ref[level] for level in range(levels)]
     leaf_sum = product(split(g_ref[...].T), split(q_ref[...]))
     leaf_parts = split(leaf_sum)
-    climb = (blocks[0], None)
-    part_ref[0] = product(leaf_parts, climb)
+    climbs = [(blocks[0], None)]
     for level in range(1, merged):
-        climb = split(product(climb, (blocks[level], None)))
-        part_ref[level] = product(leaf_parts, climb)
+        climbs.append(split(product(climbs[-1], (blocks[level], None))))
+    part_ref[merged - 1] = product(leaf_parts, climbs[merged - 1])
     pl.semaphore_wait(barrier, len(greeted))
     scatters = [None] * merged
     for level in reversed(range(merged)):
+        if level < merged - 1:
+            part_ref[level] = product(leaf_parts, climbs[level])
         scatters[level] = scatter(level)
 
+    path = [None] * levels
+    path[levels - 1] = (blocks[levels - 1], None)
+    for level in reversed(range(levels - 1)):
+        path[level] = split(product((blocks[level], None), path[level + 1]))
     for load in loads[3:]:
         load.wait()
     triangles = [leaf_ref[...]] + [tri_ref[level].astype(F32) for level in range(levels)]
@@ -270,20 +275,10 @@
         lifts.append(lift(level, value))
         spreads[level - 1] = spread(level - 1, total)
         if level == merged:
-            for below in reversed(range(merged - 1)):
-                spreads[below] = spread(below, gathered(below, scatters[below]))
             inverse_parts = [
                 split(inverse)
                 for inverse in join_inverses(inverses, triangle_parts, rows, columns)
             ]
-            path = [None] * levels
-            path[levels - 1] = (blocks[levels - 1], None)
-            for low in reversed(range(levels - 1)):
-                path[low] = split(product((blocks[low], None), path[low + 1]))
-            ratio_sums = [
-                product(triangle_parts[low], inverse_parts[low + 1]) for low in range(levels)
-            ]
-            ratio = [split(value) for value in ratio_sums]
         for copy in lifts[-1]:
             copy.wait_recv()
         terms = [lift_ref[level - merged]]
@@ -291,29 +286,38 @@
         total = add_all(terms)
     spreads[levels - 1] = spread(levels - 1, total)
 
+    for level in reversed(range(merged - 1)):
+        spreads[level] = spread(level, gathered(level, scatters[level]))
+
     top = product(triangle_parts[levels], split(root_ref[...]), True)
-    known = []
+    cot = product(split(g_ref[...]), split(product(inverse_parts[0], path[0])), True)
+    row_parts = split(q_ref[...])
+    ratio, weight = [], []
     for level in range(levels):
+        carried = product(triangle_parts[level], inverse_parts[level + 1])
+        ratio.append(split(carried))
         through = path[level][0].astype(F32)
         if path[level][1] is not None:
             through = through + path[level][1].astype(F32)
-        carried = ratio_sums[level]
         if level < levels - 1:
             carried = product(ratio[level], path[level + 1])
-        if level == 0:
-            own_sums = leaf_parts
-        else:
-            for copy in spreads[level - 1]:
-                copy.wait_recv()
-            own_sums = split(full_ref[level - 1])
-        known.append(product(split(carried - through), own_sums))
-    cot = product(split(g_ref[...]), split(product(inverse_parts[0], path[0])), True)
-    row_parts = split(q_ref[...])
+        weight.append(split(carried - through))
+
+    def known_term(level):
+        for copy in spreads[level - 1]:
+            copy.wait_recv()
+        return product(weight[level], split(full_ref[level - 1]))
+
+    known = [product(weight[0], leaf_parts)] + [None] * (levels - 1)
+    for level in range(merged, levels):
+        known[level] = known_term(level)
 
     for copy in spreads[levels - 1]:
         copy.wait_recv()
     middle = top - full_ref[levels - 1]
     for level in reversed(range(levels)):
+        if known[level] is None:
+            known[level] = known_term(level)
         mirrored = split(mirror_lower(middle, rows, columns))
         turned = product(mirrored, (blocks[level], None), True)
         middle = known[level] + product(ratio[level], split(turned))

time: 20.8 us -> 21.3 us (1.024)
  Pallas kernels: 20 us -> 20.5 us
    pallas_call x1, Pallas kernels: 20 us -> 20.5 us  [on_device(): pl.pallas_call(functools.partial(kernel, n_outer, n_inner), out_shape=jax...]
where the time goes in v5:
time: 21.3 us; the launch traced here: 21.2 us
  Pallas kernels  20.5 us (96%)
  local copies, waits for them, and re-layouts  0.66 us (3%)
    pallas_call x1, Pallas kernels, on_device(): pl.pallas_call(functools.partial(kernel, n_outer, n_inner), out_shape=jax...  20.5 us
    unnamed x1, local copies, waits for them, and re-layouts  0.66 us

profile of v5, /device:TPU:0, one launch (start us, length us, event | category | flops | bytes accessed | tf_op | source)
XLA Modules:
  0.0 21.2 jit_solution(699056230942186909)
XLA Ops:
  0.0 20.5 %shard_map.64 = f32[256,128]{1,0:T(8,128)S(1)} custom-call(f32[256,128]{1,0:T(8,128)} %q_hbm.1, f32[256,128]{1,0:T(8,128)} %g_hbm.1, f32[128,128]{1,0:T(8,128)} %leaf_hbm.1, bf16[3,128,128]{2,1,0:T(8,128)(2,1)} %blocks_hbm.1, bf16[3,128,128]{2,1,0:T(8,128)(2,1)} %tri_hbm.1, f32[128,128]{1,0:T(8,128)} %root_hbm.1), custom_call_target="tpu_custom_call" | custom-call | tf_op jit(solution)/shard_map/pallas_call | solution.py:344
  20.5 0.7 %copy.8 = f32[256,128]{1,0:T(8,128)} copy(f32[256,128]{1,0:T(8,128)S(1)} %shard_map.64) | data formatting | bytes 262144

commit v6 on v5

--- a/solution.py
+++ b/solution.py
@@ -16,6 +16,14 @@
 def split(value):
     high = value.astype(BF16)
     return high, (value - high.astype(F32)).astype(BF16)
+
+
+def keep(ref, parts):
+    ref[0], ref[1] = parts
+
+
+def kept(ref):
+    return ref[0], ref[1]
 
 
 def product(left, right, turn_right=False):
@@ -141,6 +149,7 @@
     q_hbm, g_hbm, leaf_hbm, blocks_hbm, tri_hbm, root_hbm, out_ref,
     q_ref, g_ref, leaf_ref, blocks_ref, tri_ref, root_ref,
     part_ref, scatter_ref, lift_ref, land_ref, full_ref,
+    diag_ref, inverse_ref, ratio_ref, weight_ref, sums_ref, below_ref, cot_ref, top_ref,
     in_sem, scatter_send, scatter_recv, lift_send, lift_recv, full_send, full_recv,
 ):
     fanins = fan_list(n_outer, n_inner)
@@ -247,26 +256,60 @@
     blocks = [blocks_ref[level] for level in range(levels)]
     leaf_sum = product(split(g_ref[...].T), split(q_ref[...]))
     leaf_parts = split(leaf_sum)
+    keep(sums_ref, leaf_parts)
     climbs = [(blocks[0], None)]
     for level in range(1, merged):
         climbs.append(split(product(climbs[-1], (blocks[level], None))))
     part_ref[merged - 1] = product(leaf_parts, climbs[merged - 1])
+    for load in loads[3:]:
+        load.wait()
+
+    def invert_blocks():
+        triangles = [leaf_ref[...]] + [tri_ref[level].astype(F32) for level in range(levels)]
+        for k, inverse in enumerate(block_inverses(triangles, rows, columns)):
+            diag_ref[k] = inverse
+
+    def triangle_parts():
+        return [split(leaf_ref[...])] + [(tri_ref[level], None) for level in range(levels)]
+
+    def invert():
+        inverses = [diag_ref[k] for k in range(levels + 1)]
+        for k, inverse in enumerate(join_inverses(inverses, triangle_parts(), rows, columns)):
+            keep(inverse_ref.at[k], split(inverse))
+
+    def prepare():
+        parts = triangle_parts()
+        path = [None] * levels
+        path[levels - 1] = (blocks_ref[levels - 1], None)
+        for level in reversed(range(levels - 1)):
+            path[level] = split(product((blocks_ref[level], None), path[level + 1]))
+        for level in range(levels):
+            carried = product(parts[level], kept(inverse_ref.at[level + 1]))
+            ratio = split(carried)
+            keep(ratio_ref.at[level], ratio)
+            through = path[level][0].astype(F32)
+            if path[level][1] is not None:
+                through = through + path[level][1].astype(F32)
+            if level < levels - 1:
+                carried = product(ratio, path[level + 1])
+            weight = split(carried - through)
+            if level == 0:
+                below_ref[...] = product(weight, kept(sums_ref))
+            else:
+                keep(weight_ref.at[level], weight)
+        top_ref[...] = product(parts[levels], split(root_ref[...]), True)
+        cot_path = split(product(kept(inverse_ref.at[0]), path[0]))
+        cot_ref[...] = product(split(g_ref[...]), cot_path, True)
+
+    ahead = inner < n_inner // 2
+    pl.when(ahead)(invert_blocks)
     pl.semaphore_wait(barrier, len(greeted))
     scatters = [None] * merged
     for level in reversed(range(merged)):
         if level < merged - 1:
             part_ref[level] = product(leaf_parts, climbs[level])
         scatters[level] = scatter(level)
-
-    path = [None] * levels
-    path[levels - 1] = (blocks[levels - 1], None)
-    for level in reversed(range(levels - 1)):
-        path[level] = split(product((blocks[level], None), path[level + 1]))
-    for load in loads[3:]:
-        load.wait()
-    triangles = [leaf_ref[...]] + [tri_ref[level].astype(F32) for level in range(levels)]
-    triangle_parts = [split(triangles[0])] + [(tri_ref[level], None) for level in range(levels)]
-    inverses = block_inverses(triangles, rows, columns)
+    pl.when(ahead)(invert)
 
     lifts, spreads = [], [None] * levels
     total = gathered(merged - 1, scatters[merged - 1])
@@ -275,10 +318,9 @@
         lifts.append(lift(level, value))
         spreads[level - 1] = spread(level - 1, total)
         if level == merged:
-            inverse_parts = [
-                split(inverse)
-                for inverse in join_inverses(inverses, triangle_parts, rows, columns)
-            ]
+            for below in reversed(range(merged - 1)):
+                spreads[below] = spread(below, gathered(below, scatters[below]))
+            pl.when(ahead)(prepare)
         for copy in lifts[-1]:
             copy.wait_recv()
         terms = [lift_ref[level - merged]]
@@ -286,44 +328,31 @@
         total = add_all(terms)
     spreads[levels - 1] = spread(levels - 1, total)
 
-    for level in reversed(range(merged - 1)):
-        spreads[level] = spread(level, gathered(level, scatters[level]))
-
-    top = product(triangle_parts[levels], split(root_ref[...]), True)
-    cot = product(split(g_ref[...]), split(product(inverse_parts[0], path[0])), True)
+    @pl.when(jnp.logical_not(ahead))
+    def work_late():
+        invert_blocks()
+        invert()
+        prepare()
+
+    for level in range(levels - 1):
+        for copy in spreads[level]:
+            copy.wait_recv()
+    known = [below_ref[...]]
+    for level in range(1, levels):
+        known.append(product(kept(weight_ref.at[level]), split(full_ref[level - 1])))
     row_parts = split(q_ref[...])
-    ratio, weight = [], []
-    for level in range(levels):
-        carried = product(triangle_parts[level], inverse_parts[level + 1])
-        ratio.append(split(carried))
-        through = path[level][0].astype(F32)
-        if path[level][1] is not None:
-            through = through + path[level][1].astype(F32)
-        if level < levels - 1:
-            carried = product(ratio[level], path[level + 1])
-        weight.append(split(carried - through))
-
-    def known_term(level):
-        for copy in spreads[level - 1]:
-            copy.wait_recv()
-        return product(weight[level], split(full_ref[level - 1]))
-
-    known = [product(weight[0], leaf_parts)] + [None] * (levels - 1)
-    for level in range(merged, levels):
-        known[level] = known_term(level)
+    ratio = [kept(ratio_ref.at[level]) for level in range(levels)]
 
     for copy in spreads[levels - 1]:
         copy.wait_recv()
-    middle = top - full_ref[levels - 1]
+    middle = top_ref[...] - full_ref[levels - 1]
     for level in reversed(range(levels)):
-        if known[level] is None:
-            known[level] = known_term(level)
         mirrored = split(mirror_lower(middle, rows, columns))
         turned = product(mirrored, (blocks[level], None), True)
         middle = known[level] + product(ratio[level], split(turned))
     mirrored = split(mirror_lower(middle, rows, columns))
-    solved = split(product(mirrored, inverse_parts[0], True))
-    out_ref[...] = cot + product(row_parts, solved)
+    solved = split(product(mirrored, kept(inverse_ref.at[0]), True))
+    out_ref[...] = cot_ref[...] + product(row_parts, solved)
 
     for copies in scatters + lifts + spreads:
         for copy in copies:
@@ -353,6 +382,14 @@
             pltpu.VMEM((lifted, order // groups[-1], order), F32),
             pltpu.VMEM((lifted, widest, order // groups[-1], order), F32),
             pltpu.VMEM((levels, order, order), F32),
+            pltpu.VMEM((levels + 1, BLOCK, order), F32),
+            pltpu.VMEM((levels + 1, 2, order, order), BF16),
+            pltpu.VMEM((levels, 2, order, order), BF16),
+            pltpu.VMEM((levels, 2, order, order), BF16),
+            pltpu.VMEM((2, order, order), BF16),
+            pltpu.VMEM((order, order), F32),
+            pltpu.VMEM(leaf_q.shape, F32),
+            pltpu.VMEM((order, order), F32),
             dma((len(args),)),
             dma((merged, near)),
             dma((merged, near)),

time: 21.3 us -> 20.8 us (0.977)
  Pallas kernels: 20.5 us -> 20 us
    pallas_call x1, Pallas kernels: 20.5 us -> 20 us  [on_device(): pl.pallas_call(functools.partial(kernel, n_outer, n_inner), out_shape=jax...]
where the time goes in v6:
time: 20.8 us; the launch traced here: 20.7 us
  Pallas kernels  20 us (96%)
  local copies, waits for them, and re-layouts  0.66 us (3%)
    pallas_call x1, Pallas kernels, on_device(): pl.pallas_call(functools.partial(kernel, n_outer, n_inner), out_shape=jax...  20 us
    unnamed x1, local copies, waits for them, and re-layouts  0.66 us

profile of v6, /device:TPU:0, one launch (start us, length us, event | category | flops | bytes accessed | tf_op | source)
XLA Modules:
  0.0 20.7 jit_solution(4101041059514222815)
XLA Ops:
  0.0 20.0 %shard_map.64 = f32[256,128]{1,0:T(8,128)S(1)} custom-call(f32[256,128]{1,0:T(8,128)} %q_hbm.1, f32[256,128]{1,0:T(8,128)} %g_hbm.1, f32[128,128]{1,0:T(8,128)} %leaf_hbm.1, bf16[3,128,128]{2,1,0:T(8,128)(2,1)} %blocks_hbm.1, bf16[3,128,128]{2,1,0:T(8,128)(2,1)} %tri_hbm.1, f32[128,128]{1,0:T(8,128)} %root_hbm.1), custom_call_target="tpu_custom_call" | custom-call | tf_op jit(solution)/shard_map/pallas_call | solution.py:373
  20.0 0.7 %copy.8 = f32[256,128]{1,0:T(8,128)} copy(f32[256,128]{1,0:T(8,128)S(1)} %shard_map.64) | data formatting | bytes 262144

commit v7 on v4

--- a/solution.py
+++ b/solution.py
@@ -122,13 +122,6 @@
     return fanins
 
 
-def scatter_groups(fanins, order):
-    groups = [fanins[0]]
-    if len(fanins) > 2 and order % (8 * fanins[0] * fanins[1]) == 0:
-        groups.append(fanins[0] * fanins[1])
-    return groups
-
-
 def add_all(terms):
     while len(terms) > 1:
         pairs = [left + right for left, right in zip(terms[::2], terms[1::2])]
@@ -141,12 +134,13 @@
     q_hbm, g_hbm, leaf_hbm, blocks_hbm, tri_hbm, root_hbm, out_ref,
     q_ref, g_ref, leaf_ref, blocks_ref, tri_ref, root_ref,
     part_ref, scatter_ref, lift_ref, land_ref, full_ref,
-    in_sem, scatter_send, scatter_recv, lift_send, lift_recv, full_send, full_recv,
+    top_ref, far_ref, reach_ref,
+    in_sem, top_send, top_recv, far_send, far_recv, join_send, join_recv,
+    scatter_send, scatter_recv, lift_send, lift_recv, full_send, full_recv,
 ):
     fanins = fan_list(n_outer, n_inner)
     levels = len(fanins)
-    groups = scatter_groups(fanins, leaf_ref.shape[1])
-    merged = len(groups)
+    groups, merged = [fanins[0]], 1
     outer, inner = lax.axis_index("outer"), lax.axis_index("inner")
     order = leaf_ref.shape[1]
 
@@ -165,6 +159,22 @@
         other = lax.rem(mine + step, fanins[level])
         return (outer, inner + (other - mine) * stride)
 
+    beside = min(2, n_inner)
+    team = n_outer * beside
+    team_rows = order // team
+    others = n_inner // beside
+
+    def team_place(step):
+        mine = outer * beside + lax.rem(inner, beside)
+        other = lax.rem(mine + step, team)
+        return other, (other // beside, inner - lax.rem(inner, beside) + lax.rem(other, beside))
+
+    def far_device(step):
+        return (outer, lax.rem(inner + beside * step, n_inner))
+
+    def team_slice(place):
+        return pl.ds(pl.multiple_of(place * team_rows, team_rows), team_rows)
+
     def own_rows(size):
         rows_each = order // size
         return pl.ds(pl.multiple_of(lax.rem(inner, size) * rows_each, rows_each), rows_each)
@@ -182,8 +192,10 @@
         load.start()
     barrier = pltpu.get_barrier_semaphore()
     greeted = [near(groups[-1], step)[1] for step in range(1, groups[-1])]
-    for level in range(merged, levels):
+    for level in range(merged, levels - 1):
         greeted += [above(level, step) for step in range(1, fanins[level])]
+    greeted += [team_place(step)[1] for step in range(1, team)]
+    greeted += [far_device(step) for step in range(1, others)]
     for device in greeted:
         pl.semaphore_signal(barrier, inc=1, device_id=device, device_id_type=MESH)
 
@@ -247,15 +259,23 @@
     blocks = [blocks_ref[level] for level in range(levels)]
     leaf_sum = product(split(g_ref[...].T), split(q_ref[...]))
     leaf_parts = split(leaf_sum)
-    climb = (blocks[0], None)
-    part_ref[0] = product(leaf_parts, climb)
-    for level in range(1, merged):
-        climb = split(product(climb, (blocks[level], None)))
-        part_ref[level] = product(leaf_parts, climb)
+    path = [None] * levels
+    path[levels - 1] = (blocks[levels - 1], None)
+    for level in reversed(range(levels - 1)):
+        path[level] = split(product((blocks[level], None), path[level + 1]))
+    top_ref[...] = product(leaf_parts, path[0])
     pl.semaphore_wait(barrier, len(greeted))
-    scatters = [None] * merged
-    for level in reversed(range(merged)):
-        scatters[level] = scatter(level)
+    shares = []
+    for step in range(1, team):
+        other, device = team_place(step)
+        shares.append(
+            send(
+                top_ref.at[team_slice(other)], reach_ref.at[step - 1],
+                top_send.at[step - 1], top_recv.at[step - 1], device,
+            )
+        )
+    part_ref[0] = product(leaf_parts, (blocks[0], None))
+    scatters = [scatter(0)]
 
     for load in loads[3:]:
         load.wait()
@@ -263,33 +283,50 @@
     triangle_parts = [split(triangles[0])] + [(tri_ref[level], None) for level in range(levels)]
     inverses = block_inverses(triangles, rows, columns)
 
-    lifts, spreads = [], [None] * levels
-    total = gathered(merged - 1, scatters[merged - 1])
-    for level in range(merged, levels):
-        value = product(split(total), (blocks[level], None))
-        lifts.append(lift(level, value))
-        spreads[level - 1] = spread(level - 1, total)
-        if level == merged:
-            for below in reversed(range(merged - 1)):
-                spreads[below] = spread(below, gathered(below, scatters[below]))
-            inverse_parts = [
-                split(inverse)
-                for inverse in join_inverses(inverses, triangle_parts, rows, columns)
-            ]
-            path = [None] * levels
-            path[levels - 1] = (blocks[levels - 1], None)
-            for low in reversed(range(levels - 1)):
-                path[low] = split(product((blocks[low], None), path[low + 1]))
-            ratio_sums = [
-                product(triangle_parts[low], inverse_parts[low + 1]) for low in range(levels)
-            ]
-            ratio = [split(value) for value in ratio_sums]
-        for copy in lifts[-1]:
+    lifts, spreads = [], [None] * (levels - 1)
+    mine = team_slice(team_place(0)[0])
+    for copy in shares:
+        copy.wait_recv()
+    far_ref[0] = add_all([top_ref[mine, :]] + [reach_ref[step] for step in range(team - 1)])
+    fars = [
+        send(
+            far_ref.at[0], far_ref.at[step],
+            far_send.at[step - 1], far_recv.at[step - 1], far_device(step),
+        )
+        for step in range(1, others)
+    ]
+    total = gathered(0, scatters[0])
+    if levels > 2:
+        lifts.append(lift(1, product(split(total), (blocks[1], None))))
+    spreads[0] = spread(0, total)
+
+    inverse_parts = [
+        split(inverse) for inverse in join_inverses(inverses, triangle_parts, rows, columns)
+    ]
+    ratio_sums = [
+        product(triangle_parts[level], inverse_parts[level + 1]) for level in range(levels)
+    ]
+    ratio = [split(value) for value in ratio_sums]
+
+    for copy in fars:
+        copy.wait_recv()
+    full_ref[levels - 1, mine, :] = add_all([far_ref[step] for step in range(others)])
+    joins = [
+        send(
+            full_ref.at[levels - 1, mine], full_ref.at[levels - 1, mine],
+            join_send.at[step - 1], join_recv.at[step - 1], team_place(step)[1],
+        )
+        for step in range(1, team)
+    ]
+    for level in range(1, levels - 1):
+        for copy in lifts[level - 1]:
             copy.wait_recv()
-        terms = [lift_ref[level - merged]]
-        terms += [land_ref[level - merged, step] for step in range(fanins[level] - 1)]
+        terms = [lift_ref[level - 1]]
+        terms += [land_ref[level - 1, step] for step in range(fanins[level] - 1)]
         total = add_all(terms)
-    spreads[levels - 1] = spread(levels - 1, total)
+        if level + 1 < levels - 1:
+            lifts.append(lift(level + 1, product(split(total), (blocks[level + 1], None))))
+        spreads[level] = spread(level, total)
 
     top = product(triangle_parts[levels], split(root_ref[...]), True)
     known = []
@@ -310,7 +347,7 @@
     cot = product(split(g_ref[...]), split(product(inverse_parts[0], path[0])), True)
     row_parts = split(q_ref[...])
 
-    for copy in spreads[levels - 1]:
+    for copy in joins:
         copy.wait_recv()
     middle = top - full_ref[levels - 1]
     for level in reversed(range(levels)):
@@ -321,7 +358,7 @@
     solved = split(product(mirrored, inverse_parts[0], True))
     out_ref[...] = cot + product(row_parts, solved)
 
-    for copies in scatters + lifts + spreads:
+    for copies in scatters + lifts + spreads + [shares, fars, joins]:
         for copy in copies:
             copy.wait_send()
 
@@ -330,10 +367,11 @@
     fanins = fan_list(n_outer, n_inner)
     levels = len(fanins)
     order = leaf_tri.shape[1]
-    groups = scatter_groups(fanins, order)
-    merged = len(groups)
-    lifted = levels - merged
-    widest = max(fanins[merged:]) - 1
+    groups, merged = [fanins[0]], 1
+    lifted = max(levels - 2, 1)
+    widest = max(fanins[1:-1] + [2]) - 1
+    team = n_outer * min(2, n_inner)
+    others = n_inner // min(2, n_inner)
     near = groups[-1] - 1
     dma = pltpu.SemaphoreType.DMA
     args = (leaf_q, q_cot, leaf_tri, node_blocks, node_tri, root_cot)
@@ -349,7 +387,16 @@
             pltpu.VMEM((lifted, order // groups[-1], order), F32),
             pltpu.VMEM((lifted, widest, order // groups[-1], order), F32),
             pltpu.VMEM((levels, order, order), F32),
+            pltpu.VMEM((order, order), F32),
+            pltpu.VMEM((others, order // team, order), F32),
+            pltpu.VMEM((team - 1, order // team, order), F32),
             dma((len(args),)),
+            dma((team - 1,)),
+            dma((team - 1,)),
+            dma((max(others - 1, 1),)),
+            dma((max(others - 1, 1),)),
+            dma((team - 1,)),
+            dma((team - 1,)),
             dma((merged, near)),
             dma((merged, near)),
             dma((lifted, widest)),

time: 20.8 us -> 19.6 us (0.942)
  Pallas kernels: 20 us -> 18.7 us
    pallas_call x1, Pallas kernels: 20 us -> 18.7 us  [on_device(): pl.pallas_call(functools.partial(kernel, n_outer, n_inner), out_shape=jax...]
where the time goes in v7:
time: 19.6 us; the launch traced here: 19.4 us
  Pallas kernels  18.7 us (95%)
  local copies, waits for them, and re-layouts  0.66 us (3%)
    pallas_call x1, Pallas kernels, on_device(): pl.pallas_call(functools.partial(kernel, n_outer, n_inner), out_shape=jax...  18.7 us
    unnamed x1, local copies, waits for them, and re-layouts  0.66 us

profile of v7, /device:TPU:0, one launch (start us, length us, event | category | flops | bytes accessed | tf_op | source)
XLA Modules:
  0.0 19.4 jit_solution(7722625565478196569)
XLA Ops:
  0.0 18.7 %shard_map.64 = f32[256,128]{1,0:T(8,128)S(1)} custom-call(f32[256,128]{1,0:T(8,128)} %q_hbm.1, f32[256,128]{1,0:T(8,128)} %g_hbm.1, f32[128,128]{1,0:T(8,128)} %leaf_hbm.1, bf16[3,128,128]{2,1,0:T(8,128)(2,1)} %blocks_hbm.1, bf16[3,128,128]{2,1,0:T(8,128)(2,1)} %tri_hbm.1, f32[128,128]{1,0:T(8,128)} %root_hbm.1), custom_call_target="tpu_custom_call" | custom-call | tf_op jit(solution)/shard_map/pallas_call | solution.py:378
  18.8 0.7 %copy.8 = f32[256,128]{1,0:T(8,128)} copy(f32[256,128]{1,0:T(8,128)S(1)} %shard_map.64) | data formatting | bytes 262144

commit v8 on v7

--- a/solution.py
+++ b/solution.py
@@ -329,7 +329,7 @@
         spreads[level] = spread(level, total)
 
     top = product(triangle_parts[levels], split(root_ref[...]), True)
-    known = []
+    weight = []
     for level in range(levels):
         through = path[level][0].astype(F32)
         if path[level][1] is not None:
@@ -337,20 +337,26 @@
         carried = ratio_sums[level]
         if level < levels - 1:
             carried = product(ratio[level], path[level + 1])
-        if level == 0:
-            own_sums = leaf_parts
-        else:
-            for copy in spreads[level - 1]:
-                copy.wait_recv()
-            own_sums = split(full_ref[level - 1])
-        known.append(product(split(carried - through), own_sums))
+        weight.append(split(carried - through))
+
+    def known_term(level):
+        for copy in spreads[level - 1]:
+            copy.wait_recv()
+        return product(weight[level], split(full_ref[level - 1]))
+
+    known = [product(weight[0], leaf_parts), known_term(1)] + [None] * (levels - 2)
     cot = product(split(g_ref[...]), split(product(inverse_parts[0], path[0])), True)
     row_parts = split(q_ref[...])
 
+    for copies in scatters + lifts + [shares, fars, joins]:
+        for copy in copies:
+            copy.wait_send()
     for copy in joins:
         copy.wait_recv()
     middle = top - full_ref[levels - 1]
     for level in reversed(range(levels)):
+        if known[level] is None:
+            known[level] = known_term(level)
         mirrored = split(mirror_lower(middle, rows, columns))
         turned = product(mirrored, (blocks[level], None), True)
         middle = known[level] + product(ratio[level], split(turned))
@@ -358,7 +364,7 @@
     solved = split(product(mirrored, inverse_parts[0], True))
     out_ref[...] = cot + product(row_parts, solved)
 
-    for copies in scatters + lifts + spreads + [shares, fars, joins]:
+    for copies in spreads:
         for copy in copies:
             copy.wait_send()
 

time: 19.6 us -> 19.1 us (0.974)
  Pallas kernels: 18.7 us -> 18.3 us
    pallas_call x1, Pallas kernels: 18.7 us -> 18.3 us  [on_device(): pl.pallas_call(functools.partial(kernel, n_outer, n_inner), out_shape=jax...]
where the time goes in v8:
time: 19.1 us; the launch traced here: 19 us
  Pallas kernels  18.3 us (96%)
  local copies, waits for them, and re-layouts  0.66 us (3%)
    pallas_call x1, Pallas kernels, on_device(): pl.pallas_call(functools.partial(kernel, n_outer, n_inner), out_shape=jax...  18.3 us
    unnamed x1, local copies, waits for them, and re-layouts  0.66 us

profile of v8, /device:TPU:0, one launch (start us, length us, event | category | flops | bytes accessed | tf_op | source)
XLA Modules:
  0.0 19.0 jit_solution(9386936973476913816)
XLA Ops:
  0.0 18.3 %shard_map.64 = f32[256,128]{1,0:T(8,128)S(1)} custom-call(f32[256,128]{1,0:T(8,128)} %q_hbm.1, f32[256,128]{1,0:T(8,128)} %g_hbm.1, f32[128,128]{1,0:T(8,128)} %leaf_hbm.1, bf16[3,128,128]{2,1,0:T(8,128)(2,1)} %blocks_hbm.1, bf16[3,128,128]{2,1,0:T(8,128)(2,1)} %tri_hbm.1, f32[128,128]{1,0:T(8,128)} %root_hbm.1), custom_call_target="tpu_custom_call" | custom-call | tf_op jit(solution)/shard_map/pallas_call | solution.py:384
  18.3 0.7 %copy.8 = f32[256,128]{1,0:T(8,128)} copy(f32[256,128]{1,0:T(8,128)S(1)} %shard_map.64) | data formatting | bytes 262144

commit v9 on v8

--- a/solution.py
+++ b/solution.py
@@ -183,7 +183,7 @@
         pltpu.make_async_copy(source, target, in_sem.at[k])
         for k, (source, target) in enumerate(
             [
-                (g_hbm, g_ref), (q_hbm, q_ref), (blocks_hbm, blocks_ref),
+                (blocks_hbm, blocks_ref), (g_hbm, g_ref), (q_hbm, q_ref),
                 (leaf_hbm, leaf_ref), (tri_hbm, tri_ref), (root_hbm, root_ref),
             ]
         )
@@ -254,15 +254,16 @@
         ]
 
     rows, columns = places(order)
-    for load in loads[:3]:
-        load.wait()
+    loads[0].wait()
     blocks = [blocks_ref[level] for level in range(levels)]
-    leaf_sum = product(split(g_ref[...].T), split(q_ref[...]))
-    leaf_parts = split(leaf_sum)
     path = [None] * levels
     path[levels - 1] = (blocks[levels - 1], None)
     for level in reversed(range(levels - 1)):
         path[level] = split(product((blocks[level], None), path[level + 1]))
+    for load in loads[1:3]:
+        load.wait()
+    leaf_sum = product(split(g_ref[...].T), split(q_ref[...]))
+    leaf_parts = split(leaf_sum)
     top_ref[...] = product(leaf_parts, path[0])
     pl.semaphore_wait(barrier, len(greeted))
     shares = []

time: 19.1 us -> 19.1 us (level)
  no operation moved by 1% of the time
where the time goes in v9:
time: 19.1 us; the launch traced here: 18.9 us
  Pallas kernels  18.3 us (96%)
  local copies, waits for them, and re-layouts  0.66 us (3%)
    pallas_call x1, Pallas kernels, on_device(): pl.pallas_call(functools.partial(kernel, n_outer, n_inner), out_shape=jax...  18.3 us
    unnamed x1, local copies, waits for them, and re-layouts  0.66 us

profile of v9, /device:TPU:0, one launch (start us, length us, event | category | flops | bytes accessed | tf_op | source)
XLA Modules:
  0.0 18.9 jit_solution(15401656022901845659)
XLA Ops:
  0.0 18.3 %shard_map.64 = f32[256,128]{1,0:T(8,128)S(1)} custom-call(f32[256,128]{1,0:T(8,128)} %q_hbm.1, f32[256,128]{1,0:T(8,128)} %g_hbm.1, f32[128,128]{1,0:T(8,128)} %leaf_hbm.1, bf16[3,128,128]{2,1,0:T(8,128)(2,1)} %blocks_hbm.1, bf16[3,128,128]{2,1,0:T(8,128)(2,1)} %tri_hbm.1, f32[128,128]{1,0:T(8,128)} %root_hbm.1), custom_call_target="tpu_custom_call" | custom-call | tf_op jit(solution)/shard_map/pallas_call | solution.py:385
  18.3 0.7 %copy.8 = f32[256,128]{1,0:T(8,128)} copy(f32[256,128]{1,0:T(8,128)S(1)} %shard_map.64) | data formatting | bytes 262144
